TPU v7x, 32 devices: a whole 2x2x4 slice. The times are simulated.
32 devices in a mesh: width: 2 (over x), seqo: 4 (over y, core), seqi: 4 (over z).
Axes of the slice: x: 2, y: 2, z: 4, core: 2. Of those that a mesh axis runs over, the one named last changes fastest.
Arguments:
- rows_in: bfloat16 [4096, 2048], P(('seqo', 'seqi'), 'width'), may hold values from -6 to 6
- owner: int32 [4096, 1], P(('seqo', 'seqi')), may hold values from 0 to 15; in each aligned block of 256 rows (0 to 255, 256 to 511, ...) at most 32 rows name the same one
- first_blocks: bfloat16 [16, 512, 512], P(('seqo', 'seqi')), may hold values from -0.25 to 0.25
- middle_blocks: bfloat16 [512, 16, 16], P(('seqo', 'seqi')), may hold values from -1.5 to 1.5
- last_blocks: bfloat16 [16, 512, 512], P(('seqo', 'seqi')), may hold values from -0.25 to 0.25
- kernel: bfloat16 [16, 512, 2048], P(None, ('seqo', 'seqi'), 'width'), may hold values from -6 to 6
- gate_gain: float32 [2048], P('width'), may hold values from -4 to 4
- gate_bias: float32 [2048], P('width'), may hold values from -4 to 4
- cotangent: bfloat16 [8192, 2048], P(('seqo', 'seqi'), 'width'), may hold values from -6 to 6
Outputs:
- grad_rows: bfloat16 [4096, 2048], P(('seqo', 'seqi'), 'width')
- grad_middle: float32 [512, 16, 16], P(('seqo', 'seqi'), 'width')
- grad_last: float32 [16, 512, 512], P(('seqo', 'seqi'), 'width')
- grad_kernel: bfloat16 [16, 512, 2048], P(None, ('seqo', 'seqi'), 'width')
Inputs may be any that keep to these rules, and one draw needn't show every extreme that they name: Owners are numbered over seqo and then seqi. Among the rows of one block of 256 packed rows at most 32 name the same owner, and in every draw some owner is named by exactly 32 rows of some block.
All inputs are finite; a program needn't handle non-finite values.
Results may differ from a plain program's by a relative error of at most 0.015.
Values may be sent and summed in bfloat16 or wider, within the bound.
A program may use at most 64 MiB of HBM per device.

v0:
```python
import jax
import jax.numpy as jnp
from jax import lax
from jax.sharding import PartitionSpec as P


def deliver(buffer, owners):
    by_owner = buffer.reshape(owners, buffer.shape[0] // owners, buffer.shape[1])
    arrived = lax.all_to_all(by_owner, ("seqo", "seqi"), split_axis=0, concat_axis=0, tiled=True)
    return arrived.reshape(buffer.shape)


def regroup(blocks):
    arrived = lax.all_to_all(blocks, ("seqo", "seqi"), split_axis=1, concat_axis=1, tiled=True)
    return arrived


def per_device(
    rows_in,
    owner,
    first_blocks,
    middle_blocks,
    last_blocks,
    kernel,
    gate_gain,
    gate_bias,
    cotangent,
):
    outer_count = lax.axis_size("seqo")
    owners = outer_count * lax.axis_size("seqi")
    channels = rows_in.shape[1]
    slots = cotangent.shape[0]
    capacity = slots // owners
    count_a = first_blocks.shape[0]
    block_size = first_blocks.shape[1]
    narrow = block_size // owners
    outer_len = middle_blocks.shape[1]
    target = owner[:, 0]
    matches = (target[:, None] == jnp.arange(owners, dtype=jnp.int32)[None, :]).astype(jnp.int32)
    order_rank = jnp.sum(matches * jnp.cumsum(matches, axis=0), axis=1) - 1
    slot_index = target * capacity + order_rank
    outbox = jnp.zeros((slots, channels), jnp.bfloat16).at[slot_index].set(rows_in)
    seq_in = deliver(outbox, owners).reshape(count_a, block_size, channels)
    gate_open = jax.nn.sigmoid(seq_in.astype(jnp.float32) * gate_gain + gate_bias)
    upstream = cotangent.reshape(count_a, block_size, channels).astype(jnp.float32)
    grad_mixed = (upstream * gate_open).astype(jnp.bfloat16)
    grad_weighted = jnp.einsum(
        "aij,aic->ajc", last_blocks, grad_mixed, preferred_element_type=jnp.float32
    ).astype(jnp.bfloat16)
    grad_wrows = grad_weighted.reshape(count_a, owners, narrow, channels)
    mixed_first = jnp.einsum(
        "aij,ajc->aic", first_blocks, seq_in, preferred_element_type=jnp.float32
    ).astype(jnp.bfloat16)
    first_rows = mixed_first.reshape(count_a, owners, narrow, channels)
    columns_in = regroup(first_rows)
    middle_view = middle_blocks.reshape(narrow, owners, count_a, owners, count_a)
    mixed_middle = jnp.einsum(
        "btmsl,lsbc->mtbc", middle_view, columns_in, preferred_element_type=jnp.float32
    )
    kernel_view = jnp.swapaxes(kernel.reshape(owners, count_a, narrow, channels), 0, 1).astype(
        jnp.float32
    )
    weighted_cols = (mixed_middle * kernel_view).astype(jnp.bfloat16)
    weighted = regroup(weighted_cols).reshape(count_a, block_size, channels)
    grad_cols = regroup(grad_wrows)
    grad_cols_f = grad_cols.astype(jnp.float32)
    grad_kern_view = (grad_cols_f * mixed_middle).astype(jnp.bfloat16)
    grad_kernel = jnp.swapaxes(grad_kern_view, 0, 1).reshape(outer_len, narrow, channels)
    grad_mid_in = (grad_cols_f * kernel_view).astype(jnp.bfloat16)
    part_middle = jnp.einsum(
        "mtbc,lsbc->btmsl", grad_mid_in, columns_in, preferred_element_type=jnp.float32
    )
    part_middle = part_middle.reshape(narrow, outer_len, outer_len)
    grad_first_cols = jnp.einsum(
        "btmsl,mtbc->lsbc", middle_view, grad_mid_in, preferred_element_type=jnp.float32
    ).astype(jnp.bfloat16)
    grad_first_out = regroup(grad_first_cols).reshape(count_a, block_size, channels)
    mixed_last = jnp.einsum(
        "aij,ajc->aic", last_blocks, weighted, preferred_element_type=jnp.float32
    )
    part_last = jnp.einsum("aic,ajc->aij", grad_mixed, weighted, preferred_element_type=jnp.float32)
    grad_seq = jnp.einsum(
        "aij,aic->ajc", first_blocks, grad_first_out, preferred_element_type=jnp.float32
    )
    grad_seq = grad_seq + upstream * mixed_last * gate_open * (1.0 - gate_open) * gate_gain
    returned = deliver(grad_seq.astype(jnp.bfloat16).reshape(slots, channels), owners)
    grad_rows = returned[slot_index]
    grad_middle, grad_last = (
        lax.psum_scatter(
            part_middle.astype(jnp.bfloat16), "width", scatter_dimension=1, tiled=True
        ).astype(jnp.float32),
        lax.psum_scatter(
            part_last.astype(jnp.bfloat16), "width", scatter_dimension=1, tiled=True
        ).astype(jnp.float32),
    )
    return (grad_rows, grad_middle, grad_last, grad_kernel)


def solution(mesh):
    placed = (
        P(("seqo", "seqi"), "width"),
        P(("seqo", "seqi"), None),
        P(("seqo", "seqi"), None, None),
        P(("seqo", "seqi"), None, None),
        P(("seqo", "seqi"), None, None),
        P(None, ("seqo", "seqi"), "width"),
        P("width"),
        P("width"),
        P(("seqo", "seqi"), "width"),
    )
    return jax.shard_map(
        per_device,
        mesh=mesh,
        in_specs=placed,
        out_specs=(
            P(("seqo", "seqi"), "width"),
            P(("seqo", "seqi"), "width", None),
            P(("seqo", "seqi"), "width", None),
            P(None, ("seqo", "seqi"), "width"),
        ),
        check_vma=False,
    )
```

profile of v0, /device:TPU:0, one launch (start us, length us, event | category | flops | bytes accessed | tf_op | source)
XLA Modules:
  0.0 226.7 jit_solution(6792528554140521976)
XLA Ops:
  7.2 0.0 copy-start
  7.2 0.0 copy-start.5
  7.2 0.0 copy-start.6
  7.2 0.7 fusion.30
  7.9 0.6 reduce-window.6
  8.5 0.2 slice_reduce_fusion
  8.7 0.8 fusion.29
  9.5 0.7 compare_select_fusion
  10.2 2.4 %scatter_custom_fusion = bf16[512,1024]{1,0:T(8,128)(2,1)S(1)} fusion(s32[256]{0:T(256)S(1)} %bitcast.106, bf16[256,1024]{1,0:T(8,128)(2,1)} %param.9, bf16[]{:T(256)} %constant.7.clone.1), kind=kCustom, calls=%fused_computation.37 | custom fusion | bytes 1049088 | tf_op jit(solution)/shard_map/scatter | solution.py:42
  12.6 0.0 copy-start.2
  12.6 34.3 %all_to_all.30 = bf16[16,32,1024]{2,1,0:T(8,128)(2,1)S(1)} all-to-all(bf16[16,32,1024]{2,1,0:T(8,128)(2,1)S(1)} %bitcast.100), channel_id=1, replica_groups=mesh['width'=2,'seqo'=4,'seqi'=4] {'seqo','seqi'}, dimensions={0} | all-to-all | bytes 2097152 | tf_op jit(solution)/shard_map/all_to_all | solution.py:9
  46.9 0.0 copy-done.5
  46.9 0.0 copy-done.6
  46.9 0.0 copy-done.2
  46.9 0.0 copy-start.7
  46.9 0.7 fusion
  47.7 0.0 copy-start.3
  47.7 1.0 copy-done.3
  48.7 0.0 copy-done.7
  48.7 1.7 convolution_convert_fusion.2
  50.4 3.7 %all-to-all-start.1 = ((bf16[1,16,32,1024]{3,2,0,1:T(8,128)(2,1)}), bf16[1,16,32,1024]{3,2,0,1:T(8,128)(2,1)S(1)}, u32[]{:S(2)}, u32[]{:S(2)}) async-start(bf16[1,16,32,1024]{3,2,0,1:T(8,128)(2,1)} %bitcast.103), calls=%async_computation.1 | async-start | bytes 2097152 | tf_op jit(solution)/shard_map/all_to_all | solution.py:14
  54.1 0.0 copy-done
  54.1 0.0 copy-start.4
  54.1 1.7 convolution_convert_fusion.1
  55.8 25.2 %all-to-all-done.1 = bf16[1,16,32,1024]{3,2,0,1:T(8,128)(2,1)S(1)} async-done(((bf16[1,16,32,1024]{3,2,0,1:T(8,128)(2,1)}), bf16[1,16,32,1024]{3,2,0,1:T(8,128)(2,1)S(1)}, u32[]{:S(2)}, u32[]{:S(2)}) %all-to-all-start.1) | async-done | bytes 1048608 | tf_op jit(solution)/shard_map/all_to_all | solution.py:14
  81.0 4.3 %all-to-all-start.3 = ((bf16[1,16,32,1024]{3,2,0,1:T(8,128)(2,1)}), bf16[1,16,32,1024]{3,2,0,1:T(8,128)(2,1)}, u32[]{:S(2)}, u32[]{:S(2)}) async-start(bf16[1,16,32,1024]{3,2,0,1:T(8,128)(2,1)} %bitcast.102), calls=%async_computation.3 | async-start | bytes 2097152 | tf_op jit(solution)/shard_map/all_to_all | solution.py:14
  85.3 0.0 copy-done.4
  85.3 0.2 copy.38
  85.5 3.6 %fusion.9 = bf16[1,16,32,1024]{3,1,2,0:T(8,128)(2,1)S(1)} fusion(bf16[32,16,16]{2,1,0:T(8,128)(2,1)S(1)} %copy.38, bf16[16,32,1024]{2,1,0:T(8,128)(2,1)} %param.14, bf16[1,16,32,1024]{3,2,0,1:T(8,128)(2,1)S(1)} %all-to-all-done.1), kind=kOutput, calls=%fused_computation.20 | convolution fusion | flops 19398656 | bytes 3162112 | tf_op jit(solution)/shard_map/btmsl,mtbc->lsbc/dot_general | solution.py:74
  89.1 1.6 copy.35
  90.7 21.6 %all-to-all-done.3 = bf16[1,16,32,1024]{3,2,0,1:T(8,128)(2,1)} async-done(((bf16[1,16,32,1024]{3,2,0,1:T(8,128)(2,1)}), bf16[1,16,32,1024]{3,2,0,1:T(8,128)(2,1)}, u32[]{:S(2)}, u32[]{:S(2)}) %all-to-all-start.3) | async-done | bytes 1048608 | tf_op jit(solution)/shard_map/all_to_all | solution.py:14
  112.3 4.5 %all-to-all-start.2 = ((bf16[1,16,32,1024]{3,2,0,1:T(8,128)(2,1)}), bf16[1,16,32,1024]{3,2,0,1:T(8,128)(2,1)}, u32[]{:S(2)}, u32[]{:S(2)}) async-start(bf16[1,16,32,1024]{3,2,0,1:T(8,128)(2,1)} %copy.35), calls=%async_computation.2 | async-start | bytes 2097152 | tf_op jit(solution)/shard_map/all_to_all | solution.py:14
  116.8 5.8 %fusion.13 = (bf16[16,32,1024]{2,0,1:T(8,128)(2,1)}, bf16[1,16,32,1024]{3,1,2,0:T(8,128)(2,1)S(1)}) fusion(bf16[1,16,32,1024]{3,2,0,1:T(8,128)(2,1)S(1)} %all-to-all-done.1, bf16[16,32,1024]{2,1,0:T(8,128)(2,1)} %param.14, bf16[32,16,16]{2,1,0:T(8,128)(2,1)S(1)} %copy.38, bf16[1,16,32,1024]{3,2,0,1:T(8,128)(2,1)} %all-to-all-done.3), kind=kOutput, calls=%fused_computation.26 | convolution fusion | flops 19922944 | bytes 5259264 | tf_op jit(solution)/shard_map/btmsl,lsbc->mtbc/dot_general | solution.py:57
  122.6 1.6 copy.39
  124.2 19.4 %all-to-all-done.2 = bf16[1,16,32,1024]{3,2,0,1:T(8,128)(2,1)} async-done(((bf16[1,16,32,1024]{3,2,0,1:T(8,128)(2,1)}), bf16[1,16,32,1024]{3,2,0,1:T(8,128)(2,1)}, u32[]{:S(2)}, u32[]{:S(2)}) %all-to-all-start.2) | async-done | bytes 1048608 | tf_op jit(solution)/shard_map/all_to_all | solution.py:14
  143.6 4.3 %all-to-all-start.4 = ((bf16[1,16,32,1024]{3,2,0,1:T(8,128)(2,1)}), bf16[1,16,32,1024]{3,2,0,1:T(8,128)(2,1)}, u32[]{:S(2)}, u32[]{:S(2)}) async-start(bf16[1,16,32,1024]{3,2,0,1:T(8,128)(2,1)} %copy.39), calls=%async_computation.4 | async-start | bytes 2097152 | tf_op jit(solution)/shard_map/all_to_all | solution.py:14
  148.0 3.3 %fusion.20 = f32[1024,512]{0,1:T(8,128)} fusion(bf16[512,1024]{1,0:T(8,128)(2,1)} %bitcast.15, bf16[1,512,512]{2,1,0:T(8,128)(2,1)S(1)} %copy-done), kind=kOutput, calls=%fused_computation.33 | convolution fusion | flops 536870912 | bytes 3670016 | tf_op jit(solution)/shard_map/aij,aic->ajc/dot_general | solution.py:82
  151.3 23.6 %all-to-all-done.4 = bf16[1,16,32,1024]{3,2,0,1:T(8,128)(2,1)} async-done(((bf16[1,16,32,1024]{3,2,0,1:T(8,128)(2,1)}), bf16[1,16,32,1024]{3,2,0,1:T(8,128)(2,1)}, u32[]{:S(2)}, u32[]{:S(2)}) %all-to-all-start.4) | async-done | bytes 1048608 | tf_op jit(solution)/shard_map/all_to_all | solution.py:14
  174.9 4.6 %fusion.5 = bf16[512,1024]{1,0:T(8,128)(2,1)} fusion(bf16[512,1024]{1,0:T(8,128)(2,1)} %param.17, f32[1024,512]{0,1:T(8,128)} %fusion.20, bf16[512,1024]{1,0:T(8,128)(2,1)} %bitcast.25, f32[1024]{0:T(1024)S(1)} %copy-done.6, f32[1024]{0:T(1024)S(1)} %copy-done.5, bf16[512,1024]{1,0:T(8,128)(2,1)S(1)} %bitcast.99, bf16[1,512,512]{2,1,0:T(8,128)(2,1)S(1)} %copy-done.7), kind=kOutput, calls=%fused_computation.12 | convolution fusion | flops 544210944 | bytes 6823936 | tf_op jit(solution)/shard_map/aij,ajc->aic/dot_general | solution.py:78
  179.6 3.7 %all-to-all-start.5 = ((bf16[16,32,1024]{2,1,0:T(8,128)(2,1)}), bf16[16,32,1024]{2,1,0:T(8,128)(2,1)S(1)}, u32[]{:S(2)}, u32[]{:S(2)}) async-start(bf16[16,32,1024]{2,1,0:T(8,128)(2,1)} %bitcast.101), calls=%async_computation.5 | async-start | bytes 2097152 | tf_op jit(solution)/shard_map/all_to_all | solution.py:9
  183.2 0.0 reduce-scatter.3.cloned.1.call-start
  183.3 3.3 %fusion.11 = bf16[32,16,16]{1,2,0:T(8,128)(2,1)S(1)} fusion(bf16[1,16,32,1024]{3,2,0,1:T(8,128)(2,1)} %all-to-all-done.3, bf16[16,32,1024]{2,1,0:T(8,128)(2,1)} %param.14, bf16[1,16,32,1024]{3,2,0,1:T(8,128)(2,1)S(1)} %all-to-all-done.1), kind=kOutput, calls=%fused_computation.24 | convolution fusion | flops 18882560 | bytes 3162112 | tf_op jit(solution)/shard_map/mtbc,lsbc->btmsl/dot_general | solution.py:70
  186.6 0.0 copy-start.1
  186.6 0.8 copy.40
  187.4 0.0 reduce-scatter.3.cloned.1.call-update
  187.4 0.0 reduce-scatter.5.cloned.1.call-start
  187.5 3.1 %fusion.10 = bf16[1,512,512]{2,1,0:T(8,128)(2,1)} fusion(bf16[512,1024]{1,0:T(8,128)(2,1)} %copy-done.3, bf16[512,1024]{1,0:T(8,128)(2,1)} %bitcast.25), kind=kOutput, calls=%fused_computation.22 | convolution fusion | flops 537133056 | bytes 2621440 | tf_op jit(solution)/shard_map/aic,ajc->aij/dot_general | solution.py:81
  190.5 0.0 reduce-scatter.5.cloned.1.call-update
  190.6 0.0 copy-done.1
  190.6 1.5 copy.41
  192.1 6.5 %reduce-scatter.3.cloned.1.call-done = bf16[32,8,16]{0,2,1:T(8,128)(2,1)} async-done(((bf16[32,16,16]{0,2,1:T(8,128)(2,1)}), bf16[32,8,16]{0,2,1:T(8,128)(2,1)}) %reduce-scatter.3.cloned.1.call-update) | async-done | bytes 8208 | tf_op jit(solution)/shard_map/reduce_scatter | solution.py:89
  198.7 1.4 convert_element_type.107
  200.1 16.0 %reduce-scatter.5.cloned.1.call-done = bf16[1,256,512]{2,1,0:T(8,128)(2,1)} async-done(((bf16[1,512,512]{2,1,0:T(8,128)(2,1)}), bf16[1,256,512]{2,1,0:T(8,128)(2,1)}) %reduce-scatter.5.cloned.1.call-update) | async-done | bytes 262160 | tf_op jit(solution)/shard_map/reduce_scatter | solution.py:92
  216.1 1.8 convert_element_type.110
  217.9 0.0 all-to-all-done.5
  217.9 2.0 gather_fusion
  (4 shorter events, 0.1 us)
Async XLA Ops:
  7.2 46.9 %copy-start = (bf16[1,512,512]{2,1,0:T(8,128)(2,1)S(1)}, bf16[1,512,512]{2,1,0:T(8,128)(2,1)}, u32[]{:S(2)}) copy-start(bf16[1,512,512]{2,1,0:T(8,128)(2,1)} %param.11) | copy-start | bytes 1572868
  7.2 39.7 %copy-start.5 = (f32[1024]{0:T(1024)S(1)}, f32[1024]{0:T(1024)}, u32[]{:S(2)}) copy-start(f32[1024]{0:T(1024)} %param.16) | copy-start | bytes 12292
  7.2 39.7 %copy-start.6 = (f32[1024]{0:T(1024)S(1)}, f32[1024]{0:T(1024)}, u32[]{:S(2)}) copy-start(f32[1024]{0:T(1024)} %param.15) | copy-start | bytes 12292
  12.6 34.3 %copy-start.2 = (bf16[512,1024]{1,0:T(8,128)(2,1)S(1)}, bf16[512,1024]{1,0:T(8,128)(2,1)}, u32[]{:S(2)}) copy-start(bf16[512,1024]{1,0:T(8,128)(2,1)} %param.17) | copy-start | bytes 3145732
  46.9 1.7 copy-start.7
  47.7 1.0 copy-start.3
  50.4 30.6 %all-to-all-start.1 = ((bf16[1,16,32,1024]{3,2,0,1:T(8,128)(2,1)}), bf16[1,16,32,1024]{3,2,0,1:T(8,128)(2,1)S(1)}, u32[]{:S(2)}, u32[]{:S(2)}) async-start(bf16[1,16,32,1024]{3,2,0,1:T(8,128)(2,1)} %bitcast.103), calls=%async_computation.1 | async-start | bytes 2097152 | tf_op jit(solution)/shard_map/all_to_all | solution.py:14
  54.1 31.3 %copy-start.4 = (bf16[32,16,16]{0,2,1:T(8,128)(2,1)S(1)}, bf16[32,16,16]{0,2,1:T(8,128)(2,1)}, u32[]{:S(2)}) copy-start(bf16[32,16,16]{0,2,1:T(8,128)(2,1)} %param.12) | copy-start | bytes 49156
  81.0 31.3 %all-to-all-start.3 = ((bf16[1,16,32,1024]{3,2,0,1:T(8,128)(2,1)}), bf16[1,16,32,1024]{3,2,0,1:T(8,128)(2,1)}, u32[]{:S(2)}, u32[]{:S(2)}) async-start(bf16[1,16,32,1024]{3,2,0,1:T(8,128)(2,1)} %bitcast.102), calls=%async_computation.3 | async-start | bytes 2097152 | tf_op jit(solution)/shard_map/all_to_all | solution.py:14
  112.3 31.3 %all-to-all-start.2 = ((bf16[1,16,32,1024]{3,2,0,1:T(8,128)(2,1)}), bf16[1,16,32,1024]{3,2,0,1:T(8,128)(2,1)}, u32[]{:S(2)}, u32[]{:S(2)}) async-start(bf16[1,16,32,1024]{3,2,0,1:T(8,128)(2,1)} %copy.35), calls=%async_computation.2 | async-start | bytes 2097152 | tf_op jit(solution)/shard_map/all_to_all | solution.py:14
  143.6 31.3 %all-to-all-start.4 = ((bf16[1,16,32,1024]{3,2,0,1:T(8,128)(2,1)}), bf16[1,16,32,1024]{3,2,0,1:T(8,128)(2,1)}, u32[]{:S(2)}, u32[]{:S(2)}) async-start(bf16[1,16,32,1024]{3,2,0,1:T(8,128)(2,1)} %copy.39), calls=%async_computation.4 | async-start | bytes 2097152 | tf_op jit(solution)/shard_map/all_to_all | solution.py:14
  179.6 38.3 %all-to-all-start.5 = ((bf16[16,32,1024]{2,1,0:T(8,128)(2,1)}), bf16[16,32,1024]{2,1,0:T(8,128)(2,1)S(1)}, u32[]{:S(2)}, u32[]{:S(2)}) async-start(bf16[16,32,1024]{2,1,0:T(8,128)(2,1)} %bitcast.101), calls=%async_computation.5 | async-start | bytes 2097152 | tf_op jit(solution)/shard_map/all_to_all | solution.py:9
  183.2 15.5 %reduce-scatter.3.cloned.1.call-start = ((), (), s32[]{:S(2)}) async-start(), calls=%async_computation.8 | async-start | bytes 98304 | tf_op jit(solution)/shard_map/reduce_scatter | solution.py:89
  186.6 4.0 %copy-start.1 = (bf16[16,32,1024]{2,0,1:T(8,128)(2,1)S(1)}, bf16[16,32,1024]{2,0,1:T(8,128)(2,1)}, u32[]{:S(2)}) copy-start(bf16[16,32,1024]{2,0,1:T(8,128)(2,1)} %get-tuple-element.16) | copy-start | bytes 3145732
  187.4 28.7 %reduce-scatter.5.cloned.1.call-start = ((), (), s32[]{:S(2)}) async-start(), calls=%async_computation.9 | async-start | bytes 786432 | tf_op jit(solution)/shard_map/reduce_scatter | solution.py:92
Sparse Core Ops, SparseCore 0:
  187.5 11.1 reduce-scatter.2
  201.5 14.5 reduce-scatter.4
where the time goes:
time: 228 us; the launch traced here: 227 us
  waiting for transfers between devices  113 us (50%)
  blocking collectives  34.3 us (15%)
  matrix products  27.1 us (12%)
  starting transfers between devices  20.6 us (9%)
  between operations  14.2 us (6%)
  local copies, waits for them, and re-layouts  11.2 us (5%)
  other arithmetic  6.75 us (3%)
    all_to_all x4, waiting for transfers between devices, regroup(): lax.all_to_all(blocks, ('seqo', 'seqi'), split_axis=1, concat_axis=1, til...  89.9 us
    all_to_all x1, blocking collectives, deliver(): lax.all_to_all(by_owner, ('seqo', 'seqi'), split_axis=0, concat_axis=0, t...  34.3 us
    all_to_all x4, starting transfers between devices, regroup(): lax.all_to_all(blocks, ('seqo', 'seqi'), split_axis=1, concat_axis=1, til...  16.9 us
    reduce_scatter x1, waiting for transfers between devices, per_device(): lax.psum_scatter(part_last.astype(jnp.bfloat16), 'width', scatter_dimensi...  16 us
    reduce_scatter x1, waiting for transfers between devices, per_device(): lax.psum_scatter(part_middle.astype(jnp.bfloat16), 'width', scatter_dimen...  6.55 us
    dot_general x1, matrix products, per_device(): jnp.einsum('btmsl,lsbc->mtbc', middle_view, columns_in, preferred_element...  5.75 us
    dot_general x1, matrix products, per_device(): jnp.einsum('aij,ajc->aic', last_blocks, weighted, preferred_element_type=...  4.64 us
  transfers between devices with their start and end apart: 7, of which 6 were waited for; matrix products, arithmetic and copies ran while one was open for 13% of the time, Pallas kernels for 0%

commit v1 on v0

--- a/solution.py
+++ b/solution.py
@@ -1,7 +1,13 @@
+import functools
 import jax
 import jax.numpy as jnp
 from jax import lax
+from jax.experimental import pallas as pl
+from jax.experimental.pallas import tpu as pltpu
 from jax.sharding import PartitionSpec as P
+
+CHUNKS = 2
+MESH = pl.DeviceIdType.MESH
 
 
 def deliver(buffer, owners):
@@ -15,7 +21,7 @@
     return arrived
 
 
-def per_device(
+def per_device_plain(
     rows_in,
     owner,
     first_blocks,
@@ -96,6 +102,314 @@
     return (grad_rows, grad_middle, grad_last, grad_kernel)
 
 
+def dot(a, b, contract):
+    return lax.dot_general(
+        a, b, (((contract[0],), (contract[1],)), ((), ())), preferred_element_type=jnp.float32
+    )
+
+
+def iota(shape, axis):
+    return lax.broadcasted_iota(jnp.int32, shape, axis)
+
+
+def fused(
+    n_outer,
+    n_inner,
+    rows_ref,
+    owner_ref,
+    middle_ref,
+    gain_ref,
+    bias_ref,
+    first_hbm,
+    last_hbm,
+    kernel_hbm,
+    cot_hbm,
+    grad_rows_ref,
+    grad_middle_ref,
+    grad_last_ref,
+    grad_kernel_ref,
+    first_ref,
+    last_ref,
+    kernel_ref,
+    cot_ref,
+    onehot_ref,
+    mid_ref,
+    mixed_ref,
+    factor_ref,
+    part_last_ref,
+    part_mid_ref,
+    send_last,
+    recv_last,
+    send_mid,
+    recv_mid,
+    send_buf,
+    recv_buf,
+    load_sem,
+    send_sem,
+    recv_sem,
+    peer_send,
+    peer_recv,
+):
+    owners = n_outer * n_inner
+    wide = lax.axis_index("width")
+    outer = lax.axis_index("seqo")
+    inner = lax.axis_index("seqi")
+    me = outer * n_inner + inner
+    _, chunks, _, short, width = send_buf.shape
+    slots = owners * short
+    rows = rows_ref.shape[0]
+
+    def partner(turn):
+        to_outer = lax.rem(outer + lax.rem(turn, n_outer) + 1, n_outer)
+        to_inner = lax.rem(inner + turn // n_outer + 1, n_inner)
+        return to_outer, to_inner
+
+    barrier = pltpu.get_barrier_semaphore()
+
+    @pl.loop(0, owners - 1)
+    def _(turn):
+        to_outer, to_inner = partner(turn)
+        pl.semaphore_signal(
+            barrier, inc=1, device_id=(wide, to_outer, to_inner), device_id_type=MESH
+        )
+
+    pl.semaphore_signal(barrier, inc=1, device_id=(1 - wide, outer, inner), device_id_type=MESH)
+
+    loads = [
+        pltpu.make_async_copy(source, target, load_sem.at[at])
+        for at, (source, target) in enumerate(
+            (
+                (first_hbm, first_ref),
+                (last_hbm, last_ref),
+                (kernel_hbm, kernel_ref),
+                (cot_hbm, cot_ref),
+            )
+        )
+    ]
+    for load in loads:
+        load.start()
+
+    def columns(chunk):
+        return pl.ds(pl.multiple_of(chunk * width, width), width)
+
+    def exchange(phase, chunk, values):
+        blocks = values.astype(jnp.bfloat16).reshape(owners, short, width)
+        send_buf[phase, chunk] = blocks
+        recv_buf[phase, chunk, me] = send_buf[phase, chunk, me]
+
+        @pl.loop(0, owners - 1)
+        def _(turn):
+            to_outer, to_inner = partner(turn)
+            to = to_outer * n_inner + to_inner
+            pltpu.make_async_remote_copy(
+                src_ref=send_buf.at[phase, chunk, to],
+                dst_ref=recv_buf.at[phase, chunk, me],
+                send_sem=send_sem.at[phase, chunk],
+                recv_sem=recv_sem.at[phase, chunk],
+                device_id=(wide, to_outer, to_inner),
+                device_id_type=MESH,
+            ).start()
+
+    def arrived(phase, chunk):
+        part = recv_buf.at[phase, chunk, pl.ds(0, owners - 1)]
+        pltpu.make_async_copy(part, part, recv_sem.at[phase, chunk]).wait()
+        return recv_buf[phase, chunk].reshape(slots, width)
+
+    target = owner_ref[...]
+    matches = (target == iota((rows, owners), 1)).astype(jnp.float32)
+    lower = (iota((rows, rows), 0) >= iota((rows, rows), 1)).astype(jnp.bfloat16)
+    counts = dot(lower, matches.astype(jnp.bfloat16), (1, 0))
+    rank = jnp.sum(matches * counts, axis=1, keepdims=True) - 1.0
+    slot = target.astype(jnp.float32) * float(short) + rank
+    onehot_ref[...] = (slot == iota((rows, slots), 1).astype(jnp.float32)).astype(jnp.bfloat16)
+
+    pl.semaphore_wait(barrier, owners)
+
+    @pl.loop(0, chunks)
+    def _(chunk):
+        exchange(0, chunk, dot(onehot_ref[...], rows_ref[:, columns(chunk)], (0, 0)))
+
+    row, col = iota((slots, slots), 0), iota((slots, slots), 1)
+    reorder = (col == (row % short) * owners + row // short).astype(jnp.bfloat16)
+    by_outer = dot(reorder, middle_ref[...], (1, 0)).astype(jnp.bfloat16)
+    spread = (iota((owners, slots), 0) == iota((owners, slots), 1) // short).astype(jnp.bfloat16)
+    dense = dot(by_outer, spread, (1, 0))
+    mid_ref[...] = jnp.where(row % short == col % short, dense, 0.0).astype(jnp.bfloat16)
+    part_last_ref[...] = jnp.zeros_like(part_last_ref)
+    part_mid_ref[...] = jnp.zeros_like(part_mid_ref)
+    for load in loads:
+        load.wait()
+
+    @pl.loop(0, chunks)
+    def _(chunk):
+        seq = arrived(0, chunk)
+        exchange(1, chunk, dot(first_ref[0], seq, (1, 0)))
+        gain = gain_ref[:, columns(chunk)]
+        gate = jax.nn.sigmoid(seq.astype(jnp.float32) * gain + bias_ref[:, columns(chunk)])
+        upstream = cot_ref[:, columns(chunk)].astype(jnp.float32)
+        mixed = (upstream * gate).astype(jnp.bfloat16)
+        mixed_ref[:, columns(chunk)] = mixed
+        exchange(2, chunk, dot(last_ref[0], mixed, (0, 0)))
+        factor_ref[:, columns(chunk)] = upstream * gate * (1.0 - gate) * gain
+
+    @pl.loop(0, chunks)
+    def _(chunk):
+        first_cols = arrived(1, chunk)
+        middle = dot(mid_ref[...], first_cols, (1, 0))
+        taps = kernel_ref[:, :, columns(chunk)].reshape(slots, width).astype(jnp.float32)
+        exchange(3, chunk, middle * taps)
+        grad_cols = arrived(2, chunk).astype(jnp.float32)
+        grad_mid_in = (grad_cols * taps).astype(jnp.bfloat16)
+        exchange(4, chunk, dot(mid_ref[...], grad_mid_in, (0, 0)))
+        grad_kernel_ref[:, :, columns(chunk)] = (
+            (grad_cols * middle).astype(jnp.bfloat16).reshape(owners, short, width)
+        )
+        part_mid_ref[...] += dot(grad_mid_in, first_cols, (1, 1))
+
+    @pl.loop(0, chunks)
+    def _(chunk):
+        weighted = arrived(3, chunk)
+        local = dot(last_ref[0], weighted, (1, 0)) * factor_ref[:, columns(chunk)]
+        exchange(5, chunk, dot(first_ref[0], arrived(4, chunk), (0, 0)) + local)
+        part_last_ref[...] += dot(mixed_ref[:, columns(chunk)], weighted, (1, 1))
+
+    half = slots // 2
+    send_last[...] = part_last_ref[...].astype(jnp.bfloat16).reshape(2, half, slots)
+    diagonal = jnp.where(
+        iota((slots, slots), 0) % short == iota((slots, slots), 1) % short, part_mid_ref[...], 0.0
+    ).astype(jnp.bfloat16)
+    gathered = dot(diagonal, spread, (1, 1)).astype(jnp.bfloat16)
+    few = owners // 2
+    half_row, half_col = iota((half, slots), 0), iota((half, slots), 1)
+    for side in range(2):
+        pick = half_col == (half_row % few + side * few) * short + half_row // few
+        send_mid[side] = dot(pick.astype(jnp.bfloat16), gathered, (1, 0)).astype(jnp.bfloat16)
+    peers = [
+        pltpu.make_async_remote_copy(
+            src_ref=source.at[1 - wide],
+            dst_ref=landing,
+            send_sem=peer_send.at[at],
+            recv_sem=peer_recv.at[at],
+            device_id=(1 - wide, outer, inner),
+            device_id_type=MESH,
+        )
+        for at, (source, landing) in enumerate(((send_last, recv_last), (send_mid, recv_mid)))
+    ]
+    for copy in peers:
+        copy.start()
+    for copy in peers:
+        copy.wait()
+    grad_last_ref[0] = send_last[wide].astype(jnp.float32) + recv_last[...].astype(jnp.float32)
+    grad_middle_ref[...] = send_mid[wide].astype(jnp.float32) + recv_mid[...].astype(jnp.float32)
+
+    @pl.loop(0, chunks)
+    def _(chunk):
+        returned = arrived(5, chunk)
+        grad_rows_ref[:, columns(chunk)] = dot(onehot_ref[...], returned, (1, 0)).astype(
+            jnp.bfloat16
+        )
+
+    @pl.loop(0, send_buf.shape[0])
+    def _(phase):
+        @pl.loop(0, chunks)
+        def _(chunk):
+            part = send_buf.at[phase, chunk, pl.ds(0, owners - 1)]
+            pltpu.make_async_copy(part, part, send_sem.at[phase, chunk]).wait()
+
+
+def per_device(
+    rows_in,
+    owner,
+    first_blocks,
+    middle_blocks,
+    last_blocks,
+    kernel,
+    gate_gain,
+    gate_bias,
+    cotangent,
+):
+    n_outer, n_inner = lax.axis_size("seqo"), lax.axis_size("seqi")
+    owners = n_outer * n_inner
+    rows, channels = rows_in.shape
+    slots = cotangent.shape[0]
+    short = slots // owners
+    if lax.axis_size("width") != 2 or short % 16 or first_blocks.shape[0] != 1:
+        return per_device_plain(
+            rows_in,
+            owner,
+            first_blocks,
+            middle_blocks,
+            last_blocks,
+            kernel,
+            gate_gain,
+            gate_bias,
+            cotangent,
+        )
+    width = channels // CHUNKS
+    f32, bf16 = jnp.float32, jnp.bfloat16
+    in_vmem = pl.BlockSpec(memory_space=pltpu.VMEM)
+    anywhere = pl.BlockSpec(memory_space=pl.ANY)
+    grad_rows, grad_middle, grad_last, grad_kernel = pl.pallas_call(
+        functools.partial(fused, n_outer, n_inner),
+        out_shape=(
+            jax.ShapeDtypeStruct((rows, channels), bf16),
+            jax.ShapeDtypeStruct((slots // 2, owners), f32),
+            jax.ShapeDtypeStruct((1, slots // 2, slots), f32),
+            jax.ShapeDtypeStruct(kernel.shape, bf16),
+        ),
+        in_specs=[in_vmem] * 5 + [anywhere] * 4,
+        out_specs=[in_vmem] * 4,
+        scratch_shapes=[
+            pltpu.VMEM(first_blocks.shape, bf16),
+            pltpu.VMEM(last_blocks.shape, bf16),
+            pltpu.VMEM(kernel.shape, bf16),
+            pltpu.VMEM(cotangent.shape, bf16),
+            pltpu.VMEM((rows, slots), bf16),
+            pltpu.VMEM((slots, slots), bf16),
+            pltpu.VMEM((slots, channels), bf16),
+            pltpu.VMEM((slots, channels), f32),
+            pltpu.VMEM((slots, slots), f32),
+            pltpu.VMEM((slots, slots), f32),
+            pltpu.VMEM((2, slots // 2, slots), bf16),
+            pltpu.VMEM((slots // 2, slots), bf16),
+            pltpu.VMEM((2, slots // 2, owners), bf16),
+            pltpu.VMEM((slots // 2, owners), bf16),
+            pltpu.VMEM((6, CHUNKS, owners, short, width), bf16),
+            pltpu.VMEM((6, CHUNKS, owners, short, width), bf16),
+            pltpu.SemaphoreType.DMA((4,)),
+            pltpu.SemaphoreType.DMA((6, CHUNKS)),
+            pltpu.SemaphoreType.DMA((6, CHUNKS)),
+            pltpu.SemaphoreType.DMA((2,)),
+            pltpu.SemaphoreType.DMA((2,)),
+        ],
+        compiler_params=pltpu.CompilerParams(
+            collective_id=0, has_side_effects=True, vmem_limit_bytes=56 * 1024 * 1024
+        ),
+        cost_estimate=pl.CostEstimate(
+            flops=20 * slots * slots * channels,
+            bytes_accessed=16 * slots * channels,
+            transcendentals=slots * channels,
+        ),
+        name="monarch",
+    )(
+        rows_in,
+        owner,
+        middle_blocks.reshape(slots, owners),
+        gate_gain.reshape(1, channels),
+        gate_bias.reshape(1, channels),
+        first_blocks,
+        last_blocks,
+        kernel,
+        cotangent,
+    )
+    return (
+        grad_rows,
+        grad_middle.reshape(slots // owners, owners // 2, owners),
+        grad_last,
+        grad_kernel,
+    )
+
+
 def solution(mesh):
     placed = (
         P(("seqo", "seqi"), "width"),

time: 228 us -> 153 us (0.67)
  Pallas kernels: 0 us -> 144 us
  waiting for transfers between devices: 113 us -> 0 us
  blocking collectives: 34.3 us -> 0 us
  matrix products: 27.1 us -> 0 us
  starting transfers between devices: 20.6 us -> 0 us
  between operations: 14.2 us -> 0.66 us
  other arithmetic: 6.75 us -> 0 us
  local copies, waits for them, and re-layouts: 11.2 us -> 7.74 us
    pallas_call x0 -> x1, Pallas kernels: none -> 144 us  [per_device(): pl.pallas_call(functools.partial(fused, n_outer, n_inner), out_shape=(jax...]
    all_to_all x5 -> x0, waiting for transfers between devices: 89.9 us -> none  [the longest x4 89.9 us: regroup(): lax.all_to_all(blocks, ('seqo', 'seqi'), split_axis=1, concat_axis=1, til...]
    all_to_all x1 -> x0, blocking collectives: 34.3 us -> none  [deliver(): lax.all_to_all(by_owner, ('seqo', 'seqi'), split_axis=0, concat_axis=0, t...]
    dot_general x8 -> x0, matrix products: 27.1 us -> none  [the longest x1 5.75 us: per_device(): jnp.einsum('btmsl,lsbc->mtbc', middle_view, columns_in, preferred_element...]
    reduce_scatter x2 -> x0, waiting for transfers between devices: 22.6 us -> none  [the longest x1 16 us: per_device(): lax.psum_scatter(part_last.astype(jnp.bfloat16), 'width', scatter_dimensi...]
    all_to_all x5 -> x0, starting transfers between devices: 20.5 us -> none  [the longest x4 16.9 us: regroup(): lax.all_to_all(blocks, ('seqo', 'seqi'), split_axis=1, concat_axis=1, til...]
    unnamed x18 -> x14, local copies, waits for them, and re-layouts: 2.74 us -> 7.74 us
    convert_element_type x4 -> x0, other arithmetic: 4.67 us -> none  [the longest x2 3.19 us: per_device(): grad_middle, grad_last = (lax.psum_scatter(part_middle.astype(jnp.bfloat1...]
  transfers between devices with their start and end apart: 7 -> 0, of which waited for: 6 -> 0; matrix products, arithmetic and copies ran while one was open for 13% -> 0% of each run, Pallas kernels for 0% -> 0%
where the time goes in v1:
time: 153 us; the launch traced here: 152 us
  Pallas kernels  144 us (94%)
  local copies, waits for them, and re-layouts  7.74 us (5%)
    pallas_call x1, Pallas kernels, per_device(): pl.pallas_call(functools.partial(fused, n_outer, n_inner), out_shape=(jax...  144 us
    unnamed x14, local copies, waits for them, and re-layouts  7.74 us

profile of v1, /device:TPU:0, one launch (start us, length us, event | category | flops | bytes accessed | tf_op | source)
XLA Modules:
  0.0 152.3 jit_solution(14183921109822238748)
XLA Ops:
  0.6 0.0 copy-start.3
  0.6 0.7 copy-done.3
  1.3 0.0 copy-start.2
  1.3 0.8 copy.14.owner_ref
  2.1 0.0 copy-done.2
  2.2 0.8 copy.13
  3.0 143.9 %monarch.1 = (bf16[256,1024]{1,0:T(8,128)(2,1)}, f32[256,16]{1,0:T(8,128)}, f32[1,256,512]{2,1,0:T(8,128)}, bf16[16,32,1024]{2,1,0:T(8,128)(2,1)}) custom-call(bf16[256,1024]{1,0:T(8,128)(2,1)} %rows_ref.1, s32[256,1]{1,0:T(8,128)} %copy.14.owner_ref, bf16[512,16]{1,0:T(8,128)(2,1)} %bitcast.5, f32[1,1024]{1,0:T(1,128)} %bitcast.6, f32[1,1024]{1,0:T(1,128)} %bitcast.7, ...), custom_call_target="tpu_custom_call" | custom-call | flops 5368709120 | bytes 8388608 | tf_op jit(solution)/shard_map/monarch/pallas_call | solution.py:352
  146.8 0.0 copy-start.1
  146.9 1.7 %copy.15 = f32[32,8,16]{0,2,1:T(8,128)} copy(f32[32,8,16]{2,1,0:T(8,128)} %bitcast.4) | data formatting | bytes 32768
  148.5 0.0 copy-start
  148.5 2.0 %copy.19 = bf16[256,1024]{1,0:T(8,128)(2,1)} copy(bf16[256,1024]{1,0:T(8,128)(2,1)} %get-tuple-element.20) | data formatting | bytes 1048576
  150.5 0.0 copy-done.1
  150.5 0.8 copy.20
  151.3 0.0 copy-done
  151.3 1.0 copy.21
Async XLA Ops:
  0.6 0.7 copy-start.3
  1.3 0.8 copy-start.2
  146.8 3.7 %copy-start.1 = (f32[1,256,512]{2,1,0:T(8,128)S(1)}, f32[1,256,512]{2,1,0:T(8,128)}, u32[]{:S(2)}) copy-start(f32[1,256,512]{2,1,0:T(8,128)} %get-tuple-element.22) | copy-start | bytes 1572868
  148.5 2.8 %copy-start = (bf16[16,32,1024]{2,1,0:T(8,128)(2,1)S(1)}, bf16[16,32,1024]{2,1,0:T(8,128)(2,1)}, u32[]{:S(2)}) copy-start(bf16[16,32,1024]{2,1,0:T(8,128)(2,1)} %get-tuple-element.23) | copy-start | bytes 3145732

commit v2 on v1

--- a/solution.py
+++ b/solution.py
@@ -126,6 +126,8 @@
     cot_hbm,
     grad_rows_ref,
     grad_middle_ref,
+    grad_last_hbm,
+    grad_kernel_hbm,
     grad_last_ref,
     grad_kernel_ref,
     first_ref,
@@ -145,6 +147,7 @@
     send_buf,
     recv_buf,
     load_sem,
+    store_sem,
     send_sem,
     recv_sem,
     peer_send,
@@ -160,8 +163,8 @@
     rows = rows_ref.shape[0]
 
     def partner(turn):
-        to_outer = lax.rem(outer + lax.rem(turn, n_outer) + 1, n_outer)
-        to_inner = lax.rem(inner + turn // n_outer + 1, n_inner)
+        to_outer = lax.rem(outer + turn // n_inner + 1, n_outer)
+        to_inner = lax.rem(inner + lax.rem(turn, n_inner) + 1, n_inner)
         return to_outer, to_inner
 
     barrier = pltpu.get_barrier_semaphore()
@@ -216,25 +219,29 @@
         return recv_buf[phase, chunk].reshape(slots, width)
 
     target = owner_ref[...]
-    matches = (target == iota((rows, owners), 1)).astype(jnp.float32)
-    lower = (iota((rows, rows), 0) >= iota((rows, rows), 1)).astype(jnp.bfloat16)
-    counts = dot(lower, matches.astype(jnp.bfloat16), (1, 0))
-    rank = jnp.sum(matches * counts, axis=1, keepdims=True) - 1.0
+    matches = (target == iota((owners, rows), 0)).astype(jnp.float32)
+    upper = (iota((rows, rows), 0) <= iota((rows, rows), 1)).astype(jnp.bfloat16)
+    counts = dot(matches.astype(jnp.bfloat16), upper, (1, 0))
+    rank = jnp.sum(matches * counts, axis=0, keepdims=True) - 1.0
     slot = target.astype(jnp.float32) * float(short) + rank
-    onehot_ref[...] = (slot == iota((rows, slots), 1).astype(jnp.float32)).astype(jnp.bfloat16)
+    onehot_ref[...] = (slot == iota((slots, rows), 0).astype(jnp.float32)).astype(jnp.bfloat16)
 
     pl.semaphore_wait(barrier, owners)
 
     @pl.loop(0, chunks)
     def _(chunk):
-        exchange(0, chunk, dot(onehot_ref[...], rows_ref[:, columns(chunk)], (0, 0)))
-
-    row, col = iota((slots, slots), 0), iota((slots, slots), 1)
-    reorder = (col == (row % short) * owners + row // short).astype(jnp.bfloat16)
-    by_outer = dot(reorder, middle_ref[...], (1, 0)).astype(jnp.bfloat16)
-    spread = (iota((owners, slots), 0) == iota((owners, slots), 1) // short).astype(jnp.bfloat16)
-    dense = dot(by_outer, spread, (1, 0))
-    mid_ref[...] = jnp.where(row % short == col % short, dense, 0.0).astype(jnp.bfloat16)
+        exchange(0, chunk, dot(onehot_ref[...], rows_ref[:, columns(chunk)], (1, 0)))
+
+    same_position = iota((slots, slots), 0) % short == iota((slots, slots), 1) % short
+    pairs = owners * owners
+    same_outer = (iota((pairs, slots), 0) % owners == iota((pairs, slots), 1) // short).astype(
+        jnp.float32
+    )
+    spread = (iota((short, slots), 0) == iota((short, slots), 1) % short).astype(jnp.bfloat16)
+    by_pair = (dot(middle_ref[...], spread, (1, 0)) * same_outer).astype(jnp.bfloat16)
+    lift = (iota((slots, pairs), 0) // short == iota((slots, pairs), 1) // owners).astype(jnp.bfloat16)
+    dense = dot(lift, by_pair, (1, 0))
+    mid_ref[...] = jnp.where(same_position, dense, 0.0).astype(jnp.bfloat16)
     part_last_ref[...] = jnp.zeros_like(part_last_ref)
     part_mid_ref[...] = jnp.zeros_like(part_mid_ref)
     for load in loads:
@@ -273,17 +280,17 @@
         exchange(5, chunk, dot(first_ref[0], arrived(4, chunk), (0, 0)) + local)
         part_last_ref[...] += dot(mixed_ref[:, columns(chunk)], weighted, (1, 1))
 
+    store_kernel = pltpu.make_async_copy(grad_kernel_ref, grad_kernel_hbm, store_sem.at[0])
+    store_kernel.start()
+
     half = slots // 2
     send_last[...] = part_last_ref[...].astype(jnp.bfloat16).reshape(2, half, slots)
-    diagonal = jnp.where(
-        iota((slots, slots), 0) % short == iota((slots, slots), 1) % short, part_mid_ref[...], 0.0
-    ).astype(jnp.bfloat16)
-    gathered = dot(diagonal, spread, (1, 1)).astype(jnp.bfloat16)
-    few = owners // 2
-    half_row, half_col = iota((half, slots), 0), iota((half, slots), 1)
-    for side in range(2):
-        pick = half_col == (half_row % few + side * few) * short + half_row // few
-        send_mid[side] = dot(pick.astype(jnp.bfloat16), gathered, (1, 0)).astype(jnp.bfloat16)
+    diagonal = jnp.where(same_position, part_mid_ref[...], 0.0).astype(jnp.bfloat16)
+    down = (iota((pairs, slots), 0) // owners == iota((pairs, slots), 1) // short).astype(jnp.bfloat16)
+    gathered = (dot(down, diagonal, (1, 0)) * same_outer).astype(jnp.bfloat16)
+    send_mid[...] = (
+        dot(gathered, spread, (1, 1)).astype(jnp.bfloat16).reshape(2, pairs // 2, short)
+    )
     peers = [
         pltpu.make_async_remote_copy(
             src_ref=source.at[1 - wide],
@@ -300,12 +307,14 @@
     for copy in peers:
         copy.wait()
     grad_last_ref[0] = send_last[wide].astype(jnp.float32) + recv_last[...].astype(jnp.float32)
+    store_last = pltpu.make_async_copy(grad_last_ref, grad_last_hbm, store_sem.at[1])
+    store_last.start()
     grad_middle_ref[...] = send_mid[wide].astype(jnp.float32) + recv_mid[...].astype(jnp.float32)
 
     @pl.loop(0, chunks)
     def _(chunk):
         returned = arrived(5, chunk)
-        grad_rows_ref[:, columns(chunk)] = dot(onehot_ref[...], returned, (1, 0)).astype(
+        grad_rows_ref[:, columns(chunk)] = dot(onehot_ref[...], returned, (0, 0)).astype(
             jnp.bfloat16
         )
 
@@ -315,6 +324,20 @@
         def _(chunk):
             part = send_buf.at[phase, chunk, pl.ds(0, owners - 1)]
             pltpu.make_async_copy(part, part, send_sem.at[phase, chunk]).wait()
+
+    store_kernel.wait()
+    store_last.wait()
+
+
+def settle(*refs):
+    count = (len(refs) - 1) // 2
+    copies = [
+        pltpu.make_async_copy(refs[at], refs[count + at], refs[-1].at[at]) for at in range(count)
+    ]
+    for copy in copies:
+        copy.start()
+    for copy in copies:
+        copy.wait()
 
 
 def per_device(
@@ -349,22 +372,24 @@
     f32, bf16 = jnp.float32, jnp.bfloat16
     in_vmem = pl.BlockSpec(memory_space=pltpu.VMEM)
     anywhere = pl.BlockSpec(memory_space=pl.ANY)
-    grad_rows, grad_middle, grad_last, grad_kernel = pl.pallas_call(
+    results = pl.pallas_call(
         functools.partial(fused, n_outer, n_inner),
         out_shape=(
             jax.ShapeDtypeStruct((rows, channels), bf16),
-            jax.ShapeDtypeStruct((slots // 2, owners), f32),
+            jax.ShapeDtypeStruct((owners * owners // 2, short), f32),
             jax.ShapeDtypeStruct((1, slots // 2, slots), f32),
             jax.ShapeDtypeStruct(kernel.shape, bf16),
         ),
         in_specs=[in_vmem] * 5 + [anywhere] * 4,
-        out_specs=[in_vmem] * 4,
+        out_specs=[in_vmem] * 2 + [anywhere] * 2,
         scratch_shapes=[
+            pltpu.VMEM((1, slots // 2, slots), f32),
+            pltpu.VMEM(kernel.shape, bf16),
             pltpu.VMEM(first_blocks.shape, bf16),
             pltpu.VMEM(last_blocks.shape, bf16),
             pltpu.VMEM(kernel.shape, bf16),
             pltpu.VMEM(cotangent.shape, bf16),
-            pltpu.VMEM((rows, slots), bf16),
+            pltpu.VMEM((slots, rows), bf16),
             pltpu.VMEM((slots, slots), bf16),
             pltpu.VMEM((slots, channels), bf16),
             pltpu.VMEM((slots, channels), f32),
@@ -372,11 +397,12 @@
             pltpu.VMEM((slots, slots), f32),
             pltpu.VMEM((2, slots // 2, slots), bf16),
             pltpu.VMEM((slots // 2, slots), bf16),
-            pltpu.VMEM((2, slots // 2, owners), bf16),
-            pltpu.VMEM((slots // 2, owners), bf16),
+            pltpu.VMEM((2, owners * owners // 2, short), bf16),
+            pltpu.VMEM((owners * owners // 2, short), bf16),
             pltpu.VMEM((6, CHUNKS, owners, short, width), bf16),
             pltpu.VMEM((6, CHUNKS, owners, short, width), bf16),
             pltpu.SemaphoreType.DMA((4,)),
+            pltpu.SemaphoreType.DMA((2,)),
             pltpu.SemaphoreType.DMA((6, CHUNKS)),
             pltpu.SemaphoreType.DMA((6, CHUNKS)),
             pltpu.SemaphoreType.DMA((2,)),
@@ -393,8 +419,8 @@
         name="monarch",
     )(
         rows_in,
-        owner,
-        middle_blocks.reshape(slots, owners),
+        owner.reshape(1, rows),
+        middle_blocks.transpose(1, 2, 0).reshape(owners * owners, short),
         gate_gain.reshape(1, channels),
         gate_bias.reshape(1, channels),
         first_blocks,
@@ -402,12 +428,17 @@
         kernel,
         cotangent,
     )
-    return (
-        grad_rows,
-        grad_middle.reshape(slots // owners, owners // 2, owners),
-        grad_last,
-        grad_kernel,
-    )
+    grad_rows, grad_middle, grad_last, grad_kernel = pl.pallas_call(
+        settle,
+        out_shape=tuple(jax.ShapeDtypeStruct(held.shape, held.dtype) for held in results),
+        in_specs=[anywhere] * 4,
+        out_specs=[anywhere] * 4,
+        scratch_shapes=[pltpu.SemaphoreType.DMA((4,))],
+        compiler_params=pltpu.CompilerParams(vmem_limit_bytes=56 * 1024 * 1024),
+        name="settle",
+    )(*results)
+    grad_middle = grad_middle.reshape(owners // 2, owners, short).transpose(2, 0, 1)
+    return (grad_rows, grad_middle, grad_last, grad_kernel)
 
 
 def solution(mesh):

time: 153 us -> 212 us (1.39)
  Pallas kernels: 144 us -> 211 us
  local copies, waits for them, and re-layouts: 7.74 us -> 0 us
    pallas_call x0 -> x1, Pallas kernels: none -> 66.7 us  [per_device(): pl.pallas_call(settle, out_shape=tuple((jax.ShapeDtypeStruct(held.shape,...]
    unnamed x14 -> x0, local copies, waits for them, and re-layouts: 7.74 us -> none
where the time goes in v2:
time: 212 us
  Pallas kernels  211 us (100%)
    pallas_call x1, Pallas kernels, per_device(): pl.pallas_call(functools.partial(fused, n_outer, n_inner), out_shape=(jax...  145 us
    pallas_call x1, Pallas kernels, per_device(): pl.pallas_call(settle, out_shape=tuple((jax.ShapeDtypeStruct(held.shape,...  66.7 us

profile of v2, /device:TPU:0, one launch (start us, length us, event | category | flops | bytes accessed | tf_op | source)
XLA Modules:
  0.0 212.1 jit_solution(10816785222338285518)
XLA Ops:
  0.6 144.8 %monarch.1 = (bf16[256,1024]{1,0:T(8,128)(2,1)}, f32[128,32]{1,0:T(8,128)}, f32[1,256,512]{2,1,0:T(8,128)}, bf16[16,32,1024]{2,1,0:T(8,128)(2,1)}) custom-call(bf16[256,1024]{1,0:T(8,128)(2,1)} %rows_ref.1, s32[1,256]{1,0:T(1,128)} %bitcast.13, bf16[256,32]{1,0:T(8,128)(2,1)} %bitcast.9, f32[1,1024]{1,0:T(1,128)} %bitcast.11, f32[1,1024]{1,0:T(1,128)} %bitcast.12, ...), custom_call_target="tpu_custom_call" | custom-call | flops 5368709120 | bytes 8388608 | tf_op jit(solution)/shard_map/monarch/pallas_call | solution.py:375
  145.5 66.7 %settle.1 = (bf16[256,1024]{1,0:T(8,128)(2,1)}, f32[128,32]{1,0:T(8,128)}, f32[1,256,512]{2,1,0:T(8,128)}, bf16[16,32,1024]{2,1,0:T(8,128)(2,1)}) custom-call(bf16[256,1024]{1,0:T(8,128)(2,1)} %get-tuple-element.12.refs_0_, f32[128,32]{1,0:T(8,128)} %get-tuple-element.13.refs_1_, f32[1,256,512]{2,1,0:T(8,128)} %get-tuple-element.14.refs_2_, ...), custom_call_target="tpu_custom_call" | custom-call | tf_op jit(solution)/shard_map/settle/pallas_call | solution.py:431

commit v3 on v2

--- a/solution.py
+++ b/solution.py
@@ -6,7 +6,7 @@
 from jax.experimental.pallas import tpu as pltpu
 from jax.sharding import PartitionSpec as P
 
-CHUNKS = 2
+CHUNKS = 4
 MESH = pl.DeviceIdType.MESH
 
 
@@ -115,7 +115,6 @@
 def fused(
     n_outer,
     n_inner,
-    rows_ref,
     owner_ref,
     middle_ref,
     gain_ref,
@@ -124,6 +123,7 @@
     last_hbm,
     kernel_hbm,
     cot_hbm,
+    rows_hbm,
     grad_rows_ref,
     grad_middle_ref,
     grad_last_hbm,
@@ -134,6 +134,7 @@
     last_ref,
     kernel_ref,
     cot_ref,
+    rows_ref,
     onehot_ref,
     mid_ref,
     mixed_ref,
@@ -167,17 +168,6 @@
         to_inner = lax.rem(inner + lax.rem(turn, n_inner) + 1, n_inner)
         return to_outer, to_inner
 
-    barrier = pltpu.get_barrier_semaphore()
-
-    @pl.loop(0, owners - 1)
-    def _(turn):
-        to_outer, to_inner = partner(turn)
-        pl.semaphore_signal(
-            barrier, inc=1, device_id=(wide, to_outer, to_inner), device_id_type=MESH
-        )
-
-    pl.semaphore_signal(barrier, inc=1, device_id=(1 - wide, outer, inner), device_id_type=MESH)
-
     loads = [
         pltpu.make_async_copy(source, target, load_sem.at[at])
         for at, (source, target) in enumerate(
@@ -186,11 +176,22 @@
                 (last_hbm, last_ref),
                 (kernel_hbm, kernel_ref),
                 (cot_hbm, cot_ref),
+                (rows_hbm, rows_ref),
             )
         )
     ]
-    for load in loads:
-        load.start()
+    loads[4].start()
+
+    barrier = pltpu.get_barrier_semaphore()
+
+    @pl.loop(0, owners - 1)
+    def _(turn):
+        to_outer, to_inner = partner(turn)
+        pl.semaphore_signal(
+            barrier, inc=1, device_id=(wide, to_outer, to_inner), device_id_type=MESH
+        )
+
+    pl.semaphore_signal(barrier, inc=1, device_id=(1 - wide, outer, inner), device_id_type=MESH)
 
     def columns(chunk):
         return pl.ds(pl.multiple_of(chunk * width, width), width)
@@ -226,6 +227,9 @@
     slot = target.astype(jnp.float32) * float(short) + rank
     onehot_ref[...] = (slot == iota((slots, rows), 0).astype(jnp.float32)).astype(jnp.bfloat16)
 
+    for load in loads[:4]:
+        load.start()
+    loads[4].wait()
     pl.semaphore_wait(barrier, owners)
 
     @pl.loop(0, chunks)
@@ -244,7 +248,7 @@
     mid_ref[...] = jnp.where(same_position, dense, 0.0).astype(jnp.bfloat16)
     part_last_ref[...] = jnp.zeros_like(part_last_ref)
     part_mid_ref[...] = jnp.zeros_like(part_mid_ref)
-    for load in loads:
+    for load in loads[:4]:
         load.wait()
 
     @pl.loop(0, chunks)
@@ -330,14 +334,29 @@
 
 
 def settle(*refs):
-    count = (len(refs) - 1) // 2
-    copies = [
-        pltpu.make_async_copy(refs[at], refs[count + at], refs[-1].at[at]) for at in range(count)
-    ]
-    for copy in copies:
-        copy.start()
-    for copy in copies:
-        copy.wait()
+    count = (len(refs) - 2) // 3
+    sources, targets, held = refs[:count], refs[count : 2 * count], refs[2 * count : 3 * count]
+    load_sem, store_sem = refs[3 * count :]
+    loads, stores = [], []
+    for at in range(count):
+        pieces = 1 if sources[at].shape[0] == 1 else 4
+        size = sources[at].shape[0] // pieces
+        for piece in range(pieces):
+            span, turn = pl.ds(piece * size, size), len(loads)
+            here = held[at].at[span]
+            loads.append(
+                pltpu.make_async_copy(sources[at].at[span], here, load_sem.at[turn])
+            )
+            stores.append(
+                pltpu.make_async_copy(here, targets[at].at[span], store_sem.at[turn])
+            )
+    for load in loads:
+        load.start()
+    for load, store in zip(loads, stores):
+        load.wait()
+        store.start()
+    for store in stores:
+        store.wait()
 
 
 def per_device(
@@ -380,7 +399,7 @@
             jax.ShapeDtypeStruct((1, slots // 2, slots), f32),
             jax.ShapeDtypeStruct(kernel.shape, bf16),
         ),
-        in_specs=[in_vmem] * 5 + [anywhere] * 4,
+        in_specs=[in_vmem] * 4 + [anywhere] * 5,
         out_specs=[in_vmem] * 2 + [anywhere] * 2,
         scratch_shapes=[
             pltpu.VMEM((1, slots // 2, slots), f32),
@@ -389,6 +408,7 @@
             pltpu.VMEM(last_blocks.shape, bf16),
             pltpu.VMEM(kernel.shape, bf16),
             pltpu.VMEM(cotangent.shape, bf16),
+            pltpu.VMEM(rows_in.shape, bf16),
             pltpu.VMEM((slots, rows), bf16),
             pltpu.VMEM((slots, slots), bf16),
             pltpu.VMEM((slots, channels), bf16),
@@ -401,7 +421,7 @@
             pltpu.VMEM((owners * owners // 2, short), bf16),
             pltpu.VMEM((6, CHUNKS, owners, short, width), bf16),
             pltpu.VMEM((6, CHUNKS, owners, short, width), bf16),
-            pltpu.SemaphoreType.DMA((4,)),
+            pltpu.SemaphoreType.DMA((5,)),
             pltpu.SemaphoreType.DMA((2,)),
             pltpu.SemaphoreType.DMA((6, CHUNKS)),
             pltpu.SemaphoreType.DMA((6, CHUNKS)),
@@ -418,7 +438,6 @@
         ),
         name="monarch",
     )(
-        rows_in,
         owner.reshape(1, rows),
         middle_blocks.transpose(1, 2, 0).reshape(owners * owners, short),
         gate_gain.reshape(1, channels),
@@ -427,13 +446,15 @@
         last_blocks,
         kernel,
         cotangent,
+        rows_in,
     )
     grad_rows, grad_middle, grad_last, grad_kernel = pl.pallas_call(
         settle,
         out_shape=tuple(jax.ShapeDtypeStruct(held.shape, held.dtype) for held in results),
         in_specs=[anywhere] * 4,
         out_specs=[anywhere] * 4,
-        scratch_shapes=[pltpu.SemaphoreType.DMA((4,))],
+        scratch_shapes=[pltpu.VMEM(held.shape, held.dtype) for held in results]
+        + [pltpu.SemaphoreType.DMA((16,)), pltpu.SemaphoreType.DMA((16,))],
         compiler_params=pltpu.CompilerParams(vmem_limit_bytes=56 * 1024 * 1024),
         name="settle",
     )(*results)

time: 212 us -> 149 us (0.70)
  Pallas kernels: 211 us -> 148 us
    pallas_call x1, Pallas kernels: 66.7 us -> 2.79 us  [per_device(): pl.pallas_call(settle, out_shape=tuple((jax.ShapeDtypeStruct(held.shape,...]
where the time goes in v3:
time: 149 us
  Pallas kernels  148 us (99%)
    pallas_call x1, Pallas kernels, per_device(): pl.pallas_call(functools.partial(fused, n_outer, n_inner), out_shape=(jax...  145 us

profile of v3, /device:TPU:0, one launch (start us, length us, event | category | flops | bytes accessed | tf_op | source)
XLA Modules:
  0.0 148.6 jit_solution(2209014438038980926)
XLA Ops:
  0.6 145.1 %monarch.1 = (bf16[256,1024]{1,0:T(8,128)(2,1)}, f32[128,32]{1,0:T(8,128)}, f32[1,256,512]{2,1,0:T(8,128)}, bf16[16,32,1024]{2,1,0:T(8,128)(2,1)}) custom-call(s32[1,256]{1,0:T(1,128)} %bitcast.13, bf16[256,32]{1,0:T(8,128)(2,1)} %bitcast.9, f32[1,1024]{1,0:T(1,128)} %bitcast.11, f32[1,1024]{1,0:T(1,128)} %bitcast.12, bf16[1,512,512]{2,1,0:T(8,128)(2,1)} %first_hbm.1, ...), custom_call_target="tpu_custom_call" | custom-call | flops 5368709120 | bytes 8388608 | tf_op jit(solution)/shard_map/monarch/pallas_call | solution.py:394
  145.8 2.8 %settle.1 = (bf16[256,1024]{1,0:T(8,128)(2,1)}, f32[128,32]{1,0:T(8,128)}, f32[1,256,512]{2,1,0:T(8,128)}, bf16[16,32,1024]{2,1,0:T(8,128)(2,1)}) custom-call(bf16[256,1024]{1,0:T(8,128)(2,1)} %get-tuple-element.12.refs_0_, f32[128,32]{1,0:T(8,128)} %get-tuple-element.13.refs_1_, f32[1,256,512]{2,1,0:T(8,128)} %get-tuple-element.14.refs_2_, ...), custom_call_target="tpu_custom_call" | custom-call | tf_op jit(solution)/shard_map/settle/pallas_call | solution.py:451

commit v4 on v3

--- a/solution.py
+++ b/solution.py
@@ -124,10 +124,11 @@
     kernel_hbm,
     cot_hbm,
     rows_hbm,
-    grad_rows_ref,
+    grad_rows_hbm,
     grad_middle_ref,
     grad_last_hbm,
     grad_kernel_hbm,
+    grad_rows_ref,
     grad_last_ref,
     grad_kernel_ref,
     first_ref,
@@ -149,6 +150,7 @@
     recv_buf,
     load_sem,
     store_sem,
+    rows_sem,
     send_sem,
     recv_sem,
     peer_send,
@@ -232,9 +234,11 @@
     loads[4].wait()
     pl.semaphore_wait(barrier, owners)
 
-    @pl.loop(0, chunks)
-    def _(chunk):
+    def scatter_rows(chunk):
         exchange(0, chunk, dot(onehot_ref[...], rows_ref[:, columns(chunk)], (1, 0)))
+
+    scatter_rows(0)
+    scatter_rows(1)
 
     same_position = iota((slots, slots), 0) % short == iota((slots, slots), 1) % short
     pairs = owners * owners
@@ -251,8 +255,7 @@
     for load in loads[:4]:
         load.wait()
 
-    @pl.loop(0, chunks)
-    def _(chunk):
+    def mix_first(chunk):
         seq = arrived(0, chunk)
         exchange(1, chunk, dot(first_ref[0], seq, (1, 0)))
         gain = gain_ref[:, columns(chunk)]
@@ -263,8 +266,7 @@
         exchange(2, chunk, dot(last_ref[0], mixed, (0, 0)))
         factor_ref[:, columns(chunk)] = upstream * gate * (1.0 - gate) * gain
 
-    @pl.loop(0, chunks)
-    def _(chunk):
+    def mix_middle(chunk):
         first_cols = arrived(1, chunk)
         middle = dot(mid_ref[...], first_cols, (1, 0))
         taps = kernel_ref[:, :, columns(chunk)].reshape(slots, width).astype(jnp.float32)
@@ -277,12 +279,20 @@
         )
         part_mid_ref[...] += dot(grad_mid_in, first_cols, (1, 1))
 
-    @pl.loop(0, chunks)
-    def _(chunk):
+    def mix_last(chunk):
         weighted = arrived(3, chunk)
         local = dot(last_ref[0], weighted, (1, 0)) * factor_ref[:, columns(chunk)]
         exchange(5, chunk, dot(first_ref[0], arrived(4, chunk), (0, 0)) + local)
         part_last_ref[...] += dot(mixed_ref[:, columns(chunk)], weighted, (1, 1))
+
+    @pl.loop(1, chunks + 3)
+    def _(step):
+        for lag, stage in enumerate((scatter_rows, mix_first, mix_middle, mix_last)):
+            chunk = step - lag
+
+            @pl.when((chunk >= (0 if lag else 2)) & (chunk < chunks))
+            def _():
+                stage(chunk)
 
     store_kernel = pltpu.make_async_copy(grad_kernel_ref, grad_kernel_hbm, store_sem.at[0])
     store_kernel.start()
@@ -308,19 +318,32 @@
     ]
     for copy in peers:
         copy.start()
+
+    def store_rows(chunk):
+        return pltpu.make_async_copy(
+            grad_rows_ref.at[:, columns(chunk)],
+            grad_rows_hbm.at[:, columns(chunk)],
+            rows_sem.at[chunk],
+        )
+
+    def gather_rows(chunk):
+        returned = arrived(5, chunk)
+        grad_rows_ref[:, columns(chunk)] = dot(onehot_ref[...], returned, (0, 0)).astype(
+            jnp.bfloat16
+        )
+        store_rows(chunk).start()
+
+    @pl.loop(0, chunks - 1)
+    def _(chunk):
+        gather_rows(chunk)
+
     for copy in peers:
         copy.wait()
     grad_last_ref[0] = send_last[wide].astype(jnp.float32) + recv_last[...].astype(jnp.float32)
     store_last = pltpu.make_async_copy(grad_last_ref, grad_last_hbm, store_sem.at[1])
     store_last.start()
     grad_middle_ref[...] = send_mid[wide].astype(jnp.float32) + recv_mid[...].astype(jnp.float32)
-
-    @pl.loop(0, chunks)
-    def _(chunk):
-        returned = arrived(5, chunk)
-        grad_rows_ref[:, columns(chunk)] = dot(onehot_ref[...], returned, (0, 0)).astype(
-            jnp.bfloat16
-        )
+    gather_rows(chunks - 1)
 
     @pl.loop(0, send_buf.shape[0])
     def _(phase):
@@ -328,6 +351,10 @@
         def _(chunk):
             part = send_buf.at[phase, chunk, pl.ds(0, owners - 1)]
             pltpu.make_async_copy(part, part, send_sem.at[phase, chunk]).wait()
+
+    @pl.loop(0, chunks)
+    def _(chunk):
+        store_rows(chunk).wait()
 
     store_kernel.wait()
     store_last.wait()
@@ -400,8 +427,9 @@
             jax.ShapeDtypeStruct(kernel.shape, bf16),
         ),
         in_specs=[in_vmem] * 4 + [anywhere] * 5,
-        out_specs=[in_vmem] * 2 + [anywhere] * 2,
+        out_specs=[anywhere, in_vmem, anywhere, anywhere],
         scratch_shapes=[
+            pltpu.VMEM((rows, channels), bf16),
             pltpu.VMEM((1, slots // 2, slots), f32),
             pltpu.VMEM(kernel.shape, bf16),
             pltpu.VMEM(first_blocks.shape, bf16),
@@ -423,6 +451,7 @@
             pltpu.VMEM((6, CHUNKS, owners, short, width), bf16),
             pltpu.SemaphoreType.DMA((5,)),
             pltpu.SemaphoreType.DMA((2,)),
+            pltpu.SemaphoreType.DMA((CHUNKS,)),
             pltpu.SemaphoreType.DMA((6, CHUNKS)),
             pltpu.SemaphoreType.DMA((6, CHUNKS)),
             pltpu.SemaphoreType.DMA((2,)),

time: 149 us -> 150 us (level)
  Pallas kernels: 148 us -> 150 us
    pallas_call x1, Pallas kernels: 145 us -> 147 us  [per_device(): pl.pallas_call(functools.partial(fused, n_outer, n_inner), out_shape=(jax...]
where the time goes in v4:
time: 150 us
  Pallas kernels  150 us (100%)
    pallas_call x1, Pallas kernels, per_device(): pl.pallas_call(functools.partial(fused, n_outer, n_inner), out_shape=(jax...  147 us

profile of v4, /device:TPU:0, one launch (start us, length us, event | category | flops | bytes accessed | tf_op | source)
XLA Modules:
  0.0 150.3 jit_solution(11972496992080765648)
XLA Ops:
  0.6 146.8 %monarch.1 = (bf16[256,1024]{1,0:T(8,128)(2,1)}, f32[128,32]{1,0:T(8,128)}, f32[1,256,512]{2,1,0:T(8,128)}, bf16[16,32,1024]{2,1,0:T(8,128)(2,1)}) custom-call(s32[1,256]{1,0:T(1,128)} %bitcast.13, bf16[256,32]{1,0:T(8,128)(2,1)} %bitcast.9, f32[1,1024]{1,0:T(1,128)} %bitcast.11, f32[1,1024]{1,0:T(1,128)} %bitcast.12, bf16[1,512,512]{2,1,0:T(8,128)(2,1)} %first_hbm.1, ...), custom_call_target="tpu_custom_call" | custom-call | flops 5368709120 | bytes 8388608 | tf_op jit(solution)/shard_map/monarch/pallas_call | solution.py:421
  147.5 2.8 %settle.1 = (bf16[256,1024]{1,0:T(8,128)(2,1)}, f32[128,32]{1,0:T(8,128)}, f32[1,256,512]{2,1,0:T(8,128)}, bf16[16,32,1024]{2,1,0:T(8,128)(2,1)}) custom-call(bf16[256,1024]{1,0:T(8,128)(2,1)} %get-tuple-element.12.refs_0_, f32[128,32]{1,0:T(8,128)} %get-tuple-element.13.refs_1_, f32[1,256,512]{2,1,0:T(8,128)} %get-tuple-element.14.refs_2_, ...), custom_call_target="tpu_custom_call" | custom-call | tf_op jit(solution)/shard_map/settle/pallas_call | solution.py:480
